TPU v7x, 256 devices: a whole 4x4x8 slice. The times are simulated.
256 devices in a mesh: store: 8 (over x, y_hi), tensor: 32 (over z, y_lo, core).
Axes of the slice: x: 4, y: 4 (y_hi: 2, y_lo: 2; y = y_hi * 2 + y_lo), z: 8, core: 2. Of those that a mesh axis runs over, the one named last changes fastest.
Arguments:
- suffix_tokens: bfloat16 [4096, 8192], P(('store', 'tensor')), may hold values from -6 to 6
- q_weight: bfloat16 [8192, 8192], P(None, 'tensor'), may hold values from -0.125 to 0.125
- kv_weight: bfloat16 [8192, 32, 8, 8], P(None, 'tensor'), may hold values from -0.0625 to 0.0625
- out_weight: bfloat16 [8192, 8192], P('tensor'), may hold values from -0.375 to 0.375
- prefix_pool: bfloat16 [8, 256, 8, 16, 256], P('store', 'tensor'), may hold values from -80 to 80, as said below
- page_table: int32 [32, 4], replicated, may hold values from 0 to 7, as said below
- owner_index: int32 [32], replicated, may hold values from 0 to 7
- suffix_lengths: int32 [8, 4], P('store'), may hold values from 1 to 128, 384 in all within a row
Outputs:
- attended: bfloat16 [4096, 8192], P(('store', 'tensor'))
Inputs may be any that keep to these rules, and one draw needn't show every extreme that they name: `prefix_pool`: pool entries; the key halves of a few pages can be large. `page_table`: each row holds 4 distinct slots.
All inputs are finite; a program needn't handle non-finite values.
Results may differ from a plain program's by a relative error of at most 0.033.
Values may be sent and summed in bfloat16 or wider, within the bound.
A program may use at most 128 MiB of HBM per device.

v0:
```python
import jax
import jax.numpy as jnp
from jax import lax
from jax.sharding import PartitionSpec as P

HD = 128
HEADS_DEV = 2
SLAB = 128


def spread(block, axis, source):
    block = jnp.where(lax.axis_index(axis) == source, block, jnp.zeros_like(block))
    return lax.psum(block, axis)


def rotate(values, positions):
    half_width = values.shape[-1] // 2
    frequency = 1000000.0 ** (-jnp.arange(half_width, dtype=jnp.float32) * 2.0 / values.shape[-1])
    angles = positions[:, None].astype(jnp.float32) * frequency[None, :]
    cosine = jnp.cos(angles)[:, None, :]
    sine = jnp.sin(angles)[:, None, :]
    lower_half = values[..., :half_width]
    upper_half = values[..., half_width:]
    return jnp.concatenate(
        [lower_half * cosine - upper_half * sine, upper_half * cosine + lower_half * sine], -1
    )


def attend(queries, key_rows, value_rows, lengths, prefix_len, slab):
    query_count = queries.shape[1]
    scores = jnp.einsum(
        "hsd,kd->hsk", queries, key_rows, preferred_element_type=jnp.float32
    ) * queries.shape[2] ** (-0.5)
    query_index = jnp.arange(query_count, dtype=jnp.int32)
    key_index = jnp.arange(key_rows.shape[0], dtype=jnp.int32) - prefix_len
    same_slab = (key_index[None, :] // slab == query_index[:, None] // slab) & (
        key_index[None, :] <= query_index[:, None]
    )
    allowed = (key_index[None, :] < 0) | same_slab
    scores = jnp.where(allowed[None], scores, -1e30)
    row_max = jnp.max(scores, -1, keepdims=True)
    exponent = jnp.exp(scores - row_max)
    denominator = jnp.sum(exponent, -1, keepdims=True)
    weights = (exponent / denominator).astype(jnp.bfloat16)
    mixed = jnp.einsum("hsk,kd->shd", weights, value_rows, preferred_element_type=jnp.float32)
    slab_of = query_index // slab
    slab_limit = jnp.sum(
        jnp.where(
            slab_of[:, None] == jnp.arange(lengths.shape[0], dtype=jnp.int32)[None, :],
            lengths[None, :],
            0,
        ),
        1,
    )
    query_live = query_index % slab < slab_limit
    return jnp.where(query_live[:, None, None], mixed, 0.0)


def shards(
    suffix_tokens,
    q_weight,
    kv_weight,
    out_weight,
    prefix_pool,
    page_table,
    owner_index,
    suffix_lengths,
):
    devices = lax.axis_size("tensor")
    tensor_rank = lax.axis_index("tensor")
    q_width = q_weight.shape[1]
    key_heads = kv_weight.shape[2]
    column_width = kv_weight.shape[3]
    stacked = jnp.concatenate([q_weight, kv_weight.reshape(kv_weight.shape[0], -1)], 1)
    projected = jnp.dot(
        lax.all_gather(suffix_tokens, "tensor", axis=0, tiled=True),
        stacked,
        preferred_element_type=jnp.float32,
    )
    row_count = projected.shape[0]
    kv_part = (
        projected[:, q_width:].astype(jnp.bfloat16).reshape(row_count, 1, key_heads * column_width)
    )
    kv_whole = lax.all_gather(kv_part, "tensor", axis=1, tiled=True)
    kv_whole = kv_whole.reshape(row_count, devices, key_heads, column_width)
    sharing = devices // key_heads
    own_head = tensor_rank // sharing
    own_pairs = lax.dynamic_index_in_dim(kv_whole, own_head, 2, keepdims=False).reshape(
        row_count, 2 * HD
    )
    prefix_len = page_table.shape[0] * page_table.shape[1] * prefix_pool.shape[3]
    positions = prefix_len + jnp.arange(row_count, dtype=jnp.int32) % SLAB
    queries = rotate(projected[:, :q_width].reshape(row_count, HEADS_DEV, HD), positions).astype(
        jnp.bfloat16
    )
    key_rows = rotate(own_pairs[:, None, :HD].astype(jnp.float32), positions)[:, 0].astype(
        jnp.bfloat16
    )
    value_rows = own_pairs[:, HD:]
    table_row = lax.dynamic_index_in_dim(page_table, tensor_rank, 0, keepdims=False)
    chosen = jnp.take(prefix_pool[0], table_row, axis=0)
    owner_root = lax.dynamic_index_in_dim(owner_index, tensor_rank, 0, keepdims=False)
    chosen = spread(chosen, "store", owner_root)
    gathered = lax.all_gather(chosen, "tensor", axis=0, tiled=True)
    prefix = lax.dynamic_index_in_dim(gathered, own_head, 1, keepdims=False).reshape(
        prefix_len, 2 * HD
    )
    all_keys = jnp.concatenate([prefix[:, :HD], key_rows], 0)
    all_values = jnp.concatenate([prefix[:, HD:], value_rows], 0)
    mixed = attend(
        jnp.transpose(queries, (1, 0, 2)), all_keys, all_values, suffix_lengths[0], prefix_len, SLAB
    )
    heads_out = mixed.reshape(row_count, HEADS_DEV * HD).astype(jnp.bfloat16)
    summed = lax.psum_scatter(
        jnp.dot(heads_out, out_weight, preferred_element_type=jnp.float32).astype(jnp.bfloat16),
        "tensor",
        scatter_dimension=0,
        tiled=True,
    )
    return summed


def solution(mesh):
    placed = (
        P(("store", "tensor"), None),
        P(None, "tensor"),
        P(None, "tensor", None, None),
        P("tensor", None),
        P("store", "tensor", None, None, None),
        P(),
        P(),
        P("store", None),
    )
    return jax.shard_map(
        shards, mesh=mesh, in_specs=placed, out_specs=P(("store", "tensor"), None), check_vma=False
    )
```

profile of v0, /device:TPU:1, one launch (start us, length us, event | category | flops | bytes accessed | tf_op | source)
XLA Modules:
  0.0 397.8 jit_solution(5932035962088402551)
XLA Ops:
  7.4 0.9 dynamic-slice_reduce_fusion
  8.3 1.2 dynamic_slice.16
  9.6 0.6 gather_fusion
  10.8 0.8 select_select_fusion
  11.6 0.0 all-gather.7.cloned.1.call-start
  11.7 0.5 all-gather.7.cloned.1.call-update
  12.2 0.0 all-gather.5.cloned.1.call-start
  12.2 87.4 %all-reduce.2.cloned.1.call-done = bf16[4,8,16,256]{3,2,1,0:T(8,128)(2,1)} async-done(((bf16[4,8,16,256]{3,2,1,0:T(8,128)(2,1)}), bf16[4,8,16,256]{3,2,1,0:T(8,128)(2,1)}) %all-reduce.2.cloned.1.call-update) | async-done | bytes 262160 | tf_op jit(solution)/shard_map/psum | solution.py:13
  99.7 0.0 all-gather.9.cloned.1.call-start
  99.7 2.0 copy.35
  101.8 0.0 all-gather.7.cloned.1.call-done
  101.8 8.3 %fusion.12 = f32[512,320]{0,1:T(8,128)S(1)} fusion(bf16[512,8192]{1,0:T(8,128)(2,1)} %all-gather.7.cloned.1.call-done, bf16[8192,64]{1,0:T(8,128)(2,1)S(1)} %copy.35, bf16[8192,256]{1,0:T(8,128)(2,1)} %param.9), kind=kOutput, calls=%fused_computation.18 | convolution fusion | flops 2694840320 | bytes 14286848 | tf_op jit(solution)/shard_map/dot_general | solution.py:75
  110.1 0.6 slice.61
  110.8 0.0 reduce-scatter.2.cloned.1.call-start
  110.9 0.1 select_reduce_fusion
  111.0 1.8 multiply_cosine_fusion
  112.8 1.7 fusion.9
  114.6 0.2 copy.46
  114.8 0.2 copy.47
  115.0 1.9 subtract_convert_fusion
  116.9 59.4 %all-gather.5.cloned.1.call-done = bf16[128,8,16,256]{3,2,1,0:T(8,128)(2,1)} async-done(((bf16[4,8,16,256]{3,2,1,0:T(8,128)(2,1)}), bf16[128,8,16,256]{3,2,1,0:T(8,128)(2,1)}) %all-gather.5.cloned.1.call-update) | async-done | bytes 8388624 | tf_op jit(solution)/shard_map/all_gather | solution.py:104
  176.3 1.3 constant_dynamic-slice_fusion
  177.6 0.1 fusion.59
  177.7 65.2 %all-gather.9.cloned.1.call-done = bf16[512,2048]{0,1:T(8,128)(2,1)} async-done(((bf16[512,64]{0,1:T(8,128)(2,1)}), bf16[512,2048]{0,1:T(8,128)(2,1)}) %all-gather.9.cloned.1.call-update) | async-done | bytes 2097168 | tf_op jit(solution)/shard_map/all_gather | solution.py:84
  242.9 1.0 dynamic-slice_bitcast_fusion
  243.9 0.6 fusion.31
  244.5 0.1 copy.40
  244.6 0.1 copy.45
  244.7 5.1 %fusion.62 = f32[2,512]{1,0:T(2,128)S(1)} fusion(pred[512,2560]{1,0:T(8,128)(4,1)S(1)} %fusion.9, bf16[512,128]{1,0:T(8,128)(2,1)S(1)} %copy.40, bf16[2048,128]{1,0:T(8,128)(2,1)S(1)} %get-tuple-element.8, bf16[512,2,64]{2,0,1:T(8,128)(2,1)} %get-tuple-element.6, bf16[512,2,64]{2,0,1:T(8,128)(2,1)S(1)} %copy-done.1), kind=kOutput, calls=%fused_computation.94 | convolution fusion | flops 683411968 | bytes 2232320 | tf_op jit(solution)/shard_map/sub | solution.py:42
  249.9 6.3 %fusion.16 = bf16[128,2,512]{2,0,1:T(8,128)(2,1)S(1)} fusion(f32[2,512]{1,0:T(2,128)S(1)} %fusion.62, bf16[512,128]{1,0:T(8,128)(2,1)S(1)} %copy.45, bf16[2048,128]{1,0:T(8,128)(2,1)S(1)} %get-tuple-element.7, pred[512]{0:T(512)(128)(4,1)S(1)} %fusion.41, pred[512,2560]{1,0:T(8,128)(4,1)S(1)} %fusion.9, bf16[512,128]{1,0:T(8,128)(2,1)} %copy-done.2, ...), kind=kOutput, calls=%fused_computation.20 | convolution fusion | flops 1358695936 | bytes 3150336 | tf_op jit(solution)/shard_map/hsk,kd->shd/dot_general | solution.py:45
  256.2 7.8 %convolution_convert_fusion = bf16[512,8192]{1,0:T(8,128)(2,1)} fusion(bf16[512,256]{0,1:T(8,128)(2,1)S(1)} %bitcast.62, bf16[256,8192]{1,0:T(8,128)(2,1)} %param.11), kind=kOutput, calls=%fused_computation.2 | convolution fusion | flops 2151677952 | bytes 12845056 | tf_op jit(solution)/shard_map/dot_general | solution.py:115
  264.0 126.3 %reduce-scatter.2.cloned.1.call-done = bf16[16,8192]{1,0:T(8,128)(2,1)} async-done(((bf16[512,8192]{1,0:T(8,128)(2,1)}), bf16[16,8192]{1,0:T(8,128)(2,1)}) %reduce-scatter.2.cloned.1.call-update) | async-done | bytes 262160 | tf_op jit(solution)/shard_map/reduce_scatter | solution.py:114
  (26 shorter events, 0.3 us)
Async XLA Ops:
  7.4 2.2 copy-start
  7.4 92.3 %all-reduce.2.cloned.1.call-start = ((), (), s32[]{:S(2)}) async-start(), calls=%async_computation.1 | async-start | bytes 524288 | tf_op jit(solution)/shard_map/psum | solution.py:13
  11.6 90.2 %all-gather.7.cloned.1.call-start = ((), (), s32[]{:S(2)}) async-start(), calls=%async_computation.3 | async-start | bytes 8650752 | tf_op jit(solution)/shard_map/all_gather | solution.py:76
  12.2 164.1 %all-gather.5.cloned.1.call-start = ((), (), s32[]{:S(2)}) async-start(), calls=%async_computation.2 | async-start | bytes 8650752 | tf_op jit(solution)/shard_map/all_gather | solution.py:104
  99.7 143.2 %all-gather.9.cloned.1.call-start = ((), (), s32[]{:S(2)}) async-start(), calls=%async_computation.5 | async-start | bytes 2162688 | tf_op jit(solution)/shard_map/all_gather | solution.py:84
  101.8 9.1 %copy-start.3 = (s32[1,4]{1,0:T(1,128)S(1)}, s32[1,4]{1,0:T(1,128)}, u32[]{:S(2)}) copy-start(s32[1,4]{1,0:T(1,128)} %param.15) | copy-start | bytes 52
  110.8 279.5 %reduce-scatter.2.cloned.1.call-start = ((), (), s32[]{:S(2)}) async-start(), calls=%async_computation.4 | async-start | bytes 8650752 | tf_op jit(solution)/shard_map/reduce_scatter | solution.py:114
  116.9 127.8 %copy-start.1 = (bf16[512,2,64]{2,0,1:T(8,128)(2,1)S(1)}, bf16[512,2,64]{2,0,1:T(8,128)(2,1)}, u32[]{:S(2)}) copy-start(bf16[512,2,64]{2,0,1:T(8,128)(2,1)} %get-tuple-element.5) | copy-start | bytes 393220
  244.6 5.3 %copy-start.2 = (bf16[512,128]{1,0:T(8,128)(2,1)}, bf16[512,128]{1,0:T(8,128)(2,1)S(1)}, u32[]{:S(2)}) copy-start(bf16[512,128]{1,0:T(8,128)(2,1)S(1)} %copy.40) | copy-start | bytes 393220
Sparse Core Ops, SparseCore 0:
  11.7 87.8 all-reduce.1
Sparse Core Ops, SparseCore 1:
  13.9 77.1 all-gather.6
  99.8 76.5 all-gather.4
  178.2 64.7 all-gather.8
  264.1 126.1 reduce-scatter.1
where the time goes:
time: 401 us; the launch traced here: 398 us
  waiting for transfers between devices  339 us (85%)
  matrix products  27.5 us (7%)
  between operations  15.9 us (4%)
  local copies, waits for them, and re-layouts  8.46 us (2%)
  other arithmetic  6.97 us (2%)
    reduce_scatter x1, waiting for transfers between devices, shards(): lax.psum_scatter(jnp.dot(heads_out, out_weight, preferred_element_type=jn...  126 us
    psum x1, waiting for transfers between devices, spread(): return lax.psum(block, axis)  87.4 us
    all_gather x1, waiting for transfers between devices, shards(): kv_whole = lax.all_gather(kv_part, 'tensor', axis=1, tiled=True)  65.2 us
    all_gather x1, waiting for transfers between devices, shards(): gathered = lax.all_gather(chosen, 'tensor', axis=0, tiled=True)  59.4 us
    dot_general x1, matrix products, shards(): jnp.dot(lax.all_gather(suffix_tokens, 'tensor', axis=0, tiled=True), stac...  8.29 us
  transfers between devices with their start and end apart: 5, of which 4 were waited for; matrix products, arithmetic and copies ran while one was open for 5% of the time, Pallas kernels for 0%

commit v1 on v0

v1 whole, which is shorter than its diff:
```python
import jax
import jax.numpy as jnp
import numpy as np
from jax import lax
from jax.experimental import pallas as pl
from jax.experimental.pallas import tpu as pltpu
from jax.sharding import PartitionSpec as P

MESH = pl.DeviceIdType.MESH
F32 = jnp.float32
BF16 = jnp.bfloat16
HD = 128
SLAB = 128
ROW = 16
NZ = 8
PREFIX = 2048
NEG = -1e30
SCALE = 128 ** -0.5
PARTS = 2


def rope_tables():
    freq = np.float32(1000000.0) ** (-np.arange(HD // 2, dtype=np.float32) * np.float32(2.0) / np.float32(HD))
    pos = (PREFIX + np.arange(SLAB)).astype(np.float32)
    angles = (pos[:, None] * freq.astype(np.float32)[None, :]).astype(np.float32)
    cos = np.cos(angles.astype(np.float64)).astype(np.float32)
    sin = np.sin(angles.astype(np.float64)).astype(np.float32)
    by_row = np.stack([np.concatenate([cos, cos], 1), np.concatenate([-sin, sin], 1)])
    by_column = np.stack([cos.T, sin.T])
    return np.ascontiguousarray(by_row), np.ascontiguousarray(by_column)


def slab_order(zp):
    so, d = zp // 2, 2 * (zp % 2) - 1
    return [so, (so + 4 + d) % 4, (so + 4 - d) % 4, (so + 2) % 4]


def kernel(
    x_ref, qw_hbm, kvw_hbm, ow_hbm, pool_hbm, pt_ref, own_ref, len_ref, rope_ref, ropet_ref,
    out_ref,
    tok, qw, kvw, ow, pool, chosen, r1, sel, pb, kv0, kvs, kvr, lens, qs, ms, ls, accs, ho, hos,
    part, rb4, rb, rby,
    ssem, lsem, tsem, p1sem, p2sem, p3asem, p3bsem, p3csem, kvzsem, kvpsem, hosem, owsem, lensem,
    rb4sem, rbsem, rbysem,
):
    t = lax.axis_index("tensor")
    s = lax.axis_index("store")
    z, y, c = t // 4, lax.rem(t // 2, 2), lax.rem(t, 2)
    sx, yh = s // 2, lax.rem(s, 2)
    cols = x_ref.shape[1]
    wide = cols // PARTS
    parts = range(PARTS)
    cut = [pl.ds(g * wide, wide) for g in parts]

    def m8(v):
        return lax.rem(v + 16, 8)

    def tid(zz, yy, cc):
        return zz * 4 + yy * 2 + cc

    def tdev(zz, yy, cc):
        return {"tensor": tid(zz, yy, cc)}

    y4 = 2 * yh + y

    def ydev(step, cc):
        there = lax.rem(y4 + step + 4, 4)
        return {"store": sx * 2 + there // 2, "tensor": tid(z, lax.rem(there, 2), cc)}

    sib = tdev(z, y, 1 - c)
    ysend, yrecv = ydev(1 - 2 * c, c), ydev(2 * c - 1, c)
    plane = [((k, c), ydev(k, c)) for k in (1, 2, 3)] + [((k, 1 - c), ydev(k, 1 - c)) for k in range(4)]
    pending = []

    def send(src, dst, rsem, dev):
        copy = pltpu.make_async_remote_copy(
            src_ref=src, dst_ref=dst, send_sem=ssem.at[len(pending)], recv_sem=rsem,
            device_id=dev, device_id_type=MESH,
        )
        copy.start()
        pending.append(copy)

    def arrived(dst, rsem):
        pltpu.make_async_remote_copy(
            src_ref=dst, dst_ref=dst, send_sem=ssem.at[0], recv_sem=rsem,
            device_id=sib, device_id_type=MESH,
        ).wait_recv()

    own = tid(z, y, c)
    l_x = pltpu.make_async_copy(x_ref, tok.at[own], lsem.at[0])
    l_pool = pltpu.make_async_copy(pool_hbm, pool, lsem.at[1])
    l_kv = pltpu.make_async_copy(kvw_hbm, kvw, lsem.at[2])
    l_q = pltpu.make_async_copy(qw_hbm, qw, lsem.at[3])
    l_ow = pltpu.make_async_copy(ow_hbm, ow.at[0], lsem.at[4])
    l_x.start()
    l_pool.start()

    barrier = pltpu.get_barrier_semaphore()
    partners = [tdev(m8(z + k), y, c) for k in range(1, NZ)]
    partners += [{"store": lax.rem(s + k, 8)} for k in range(1, 8)]
    partners += [ysend, yrecv] + [ydev(k, 1 - c) for k in range(4)]
    for dev in partners:
        pl.semaphore_signal(barrier, inc=1, device_id=dev, device_id_type=MESH)

    l_pool.wait()
    for j in range(4):
        page = pool[pt_ref[j, t]]
        chosen[j, 0] = page[:, :, :HD]
        chosen[j, 1] = page[:, :, HD:]
    l_x.wait()
    pl.semaphore_wait(barrier, len(partners))
    l_kv.start()
    l_q.start()
    l_ow.start()

    def blk(b, h):
        return tok.at[b, :, cut[h]]

    def tsend(b, h, dev):
        send(blk(b, h), blk(b, h), tsem.at[h, b], dev)

    def twait(b, h):
        arrived(blk(b, h), tsem.at[h, b])

    up, down = tdev(m8(z + 1), y, c), tdev(m8(z - 1), y, c)
    step_dev = {1: up, -1: down}

    for g in parts:
        for dev in (up, down, ysend):
            tsend(own, g, dev)
    for k in range(1, 8):
        so = lax.rem(s + k, 8)
        send(chosen.at[so // 2, lax.rem(so, 2)], r1.at[s], p1sem.at[s], {"store": so})
    for g in parts:
        tsend(own, g, sib)
    r1[s] = chosen[sx, yh]
    for slab in range(8):
        lens[0, slab] = jnp.full((SLAB,), len_ref[0, slab % 4], jnp.int32).astype(F32)
    send(lens.at[0], lens.at[1], lensem.at[0], {"store": sx * 2 + 1 - yh})
    def z_step(k):
        for g in parts:
            turn = 1 - 2 * (g % 2)
            for d in (turn,) if k == 4 else (turn, -turn):
                b = tid(m8(z - d * k), y, c)
                twait(b, g)
                if k < 3 or (k == 3 and d == turn):
                    tsend(b, g, step_dev[d])
                tsend(b, g, ysend)
                tsend(b, g, sib)

    def y_step(k):
        for g in parts:
            for zz in [z] if k == 0 else [m8(z + 4)] if k == 4 else [m8(z - k), m8(z + k)]:
                b = tid(zz, 1 - y, c)
                twait(b, g)
                tsend(b, g, sib)

    def sib_wait(slab):
        for i in range(4):
            b = slab * 8 + i * 2 + 1 - c
            for g in parts:
                twait(b, g)

    so = z // 2
    dd = 2 * lax.rem(z, 2) - 1
    order = [so, lax.rem(so + 4 + dd, 4), lax.rem(so + 4 - dd, 4), lax.rem(so + 2, 4)]
    KC = 1024

    def rows_of(slabs, k):
        cs = pl.ds(pl.multiple_of(k * KC, KC), KC)
        rows = [tok[pl.ds(slab * 8, 8), :, cs].reshape(SLAB, KC) for slab in slabs]
        return rows[0] if len(rows) == 1 else jnp.concatenate(rows, 0)

    def kv_proj(*which):
        slabs = [order[i] for i in which]

        def body(k, acc):
            w = kvw[:, pl.ds(pl.multiple_of(k * KC, KC), KC)]
            return acc + lax.dot_general(
                rows_of(slabs, k), w, (((1,), (1,)), ((), ())), preferred_element_type=F32
            )

        res = lax.fori_loop(0, cols // KC, body, jnp.zeros((SLAB * len(slabs), 64), F32))
        return [res[i * SLAB : (i + 1) * SLAB].T for i in range(len(slabs))]

    def kv_send(m, first, second):
        for h in range(8):
            at = slice(h * 8, h * 8 + 8)
            kvs[m, h] = jnp.concatenate([first[at], second[at]], 0).astype(BF16)
        kvr[y4, c, m, z] = kvs[m, z]
        for k in range(1, NZ):
            zz = m8(z + k)
            send(kvs.at[m, zz], kvr.at[y4, c, m, z], kvzsem.at[m, z], tdev(zz, y, c))

    def kv_plane(m):
        for k in range(1, NZ):
            zz = m8(z + k)
            arrived(kvr.at[y4, c, m, zz], kvzsem.at[m, zz])
        for _, dev in plane:
            send(kvr.at[y4, c, m], kvr.at[y4, c, m], kvpsem.at[m, y4 * 2 + c], dev)

    def kv_wait(m):
        for (k, cc), _ in plane:
            yy = lax.rem(y4 + k, 4)
            arrived(kvr.at[yy, cc, m], kvpsem.at[m, yy * 2 + cc])

    def q_proj(*which):
        slabs = [order[i] for i in which]

        def body(k, acc):
            w = qw[pl.ds(pl.multiple_of(k * KC, KC), KC), :]
            return acc + jnp.dot(rows_of(slabs, k), w, preferred_element_type=F32)

        res = lax.fori_loop(0, cols // KC, body, jnp.zeros((SLAB * len(slabs), 2 * HD), F32))
        for i, slab in enumerate(slabs):
            for h in range(2):
                v = res[i * SLAB : (i + 1) * SLAB, h * HD : (h + 1) * HD]
                v = v * rope_ref[0] + pltpu.roll(v, HD // 2, 1) * rope_ref[1]
                qs[slab, pl.ds(h * SLAB, SLAB), :] = v.astype(BF16)

    def prefix_attn(i):
        slab = order[i]
        q = qs[slab]

        def body(x, carry):
            m, l, acc = carry
            keys = jnp.concatenate([pb[0, x, 0].reshape(256, HD), pb[1, x, 0].reshape(256, HD)], 0)
            vals = jnp.concatenate([pb[0, x, 1].reshape(256, HD), pb[1, x, 1].reshape(256, HD)], 0)
            sc = SCALE * lax.dot_general(
                q, keys, (((1,), (1,)), ((), ())), preferred_element_type=F32
            )
            m_new = jnp.maximum(m, jnp.max(sc, 1, keepdims=True))
            w = jnp.exp(sc - m_new)
            fix = jnp.exp(m - m_new)
            l = l * fix + jnp.sum(w, 1, keepdims=True)
            acc = acc * fix + jnp.dot(w.astype(BF16), vals, preferred_element_type=F32)
            return m_new, l, acc

        rows = 2 * SLAB
        m, l, acc = lax.fori_loop(
            0, 4, body,
            (jnp.full((rows, 1), NEG, F32), jnp.zeros((rows, 1), F32), jnp.zeros((rows, HD), F32)),
        )
        ms[slab] = jnp.broadcast_to(m, (rows, HD))
        ls[slab] = jnp.broadcast_to(l, (rows, HD))
        accs[slab] = acc

    ydevs = []
    for k in (1, 2, 3):
        there = lax.rem(y4 + k, 4)
        ydevs.append((ydev(k, c), there // 2, lax.rem(there, 2)))
    z_step(1)
    for k in range(1, 8):
        so = lax.rem(s + k, 8)
        arrived(r1.at[so], p1sem.at[so])
    sel[...] = r1[own_ref[t]]
    for k in range(1, NZ):
        zz = m8(z + k)
        send(sel.at[zz], pb.at[c, sx, yh, y, z], p2sem.at[z], tdev(zz, y, c))
    pb[c, sx, yh, y, z] = sel[z]
    y_step(0)
    z_step(2)
    for k in range(1, NZ):
        zz = m8(z + k)
        arrived(pb.at[c, sx, yh, y, zz], p2sem.at[zz])
    for dev, hh, yy in ydevs:
        send(pb.at[c, sx, yh, y], pb.at[c, sx, yh, y], p3asem.at[yh * 2 + y], dev)
    l_ow.wait()
    send(ow.at[0], ow.at[1], owsem.at[0], sib)
    y_step(1)
    z_step(3)
    for dev, hh, yy in ydevs:
        arrived(pb.at[c, sx, hh, yy], p3asem.at[hh * 2 + yy])
    for k in range(1, 4):
        xx = lax.rem(sx + k, 4)
        send(pb.at[c, sx], pb.at[c, sx], p3bsem.at[sx], {"store": xx * 2 + yh})
    y_step(2)
    l_kv.wait()
    l_q.wait()
    sib_wait(order[0])
    sib_wait(order[1])
    kv_send(0, *kv_proj(0, 1))
    q_proj(0, 1)
    for k in range(1, 4):
        xx = lax.rem(sx + k, 4)
        arrived(pb.at[c, xx], p3bsem.at[xx])
    send(pb.at[c], pb.at[c], p3csem.at[0], sib)
    z_step(4)
    y_step(3)
    arrived(pb.at[1 - c], p3csem.at[0])
    prefix_attn(0)
    sib_wait(order[2])
    kv0[...] = kv_proj(2)[0]
    y_step(4)
    q_proj(2)
    sib_wait(order[3])
    kv_send(1, kv0[...], kv_proj(3)[0])
    q_proj(3)
    kv_plane(0)
    prefix_attn(1)
    kv_plane(1)
    prefix_attn(2)
    prefix_attn(3)
    kv_wait(0)
    kv_wait(1)

    arrived(lens.at[1], lensem.at[0])
    row = lax.rem(lax.broadcasted_iota(jnp.int32, (2 * SLAB, 2 * SLAB), 0), SLAB)
    col = lax.broadcasted_iota(jnp.int32, (2 * SLAB, 2 * SLAB), 1)
    guest = lax.rem(row // ROW, 4) == 2 - y
    causal = (lax.rem(col, SLAB) <= row) & ((col >= SLAB) == guest)
    row, guest = row[:, :SLAB], guest[:, :SLAB]
    lane = lax.rem(lax.broadcasted_iota(jnp.int32, (HD, SLAB), 1) // ROW, 4)
    dim_y = lax.rem(lax.broadcasted_iota(jnp.int32, (HD, SLAB), 0) // 16, 2)
    key_guest = lane == 2 - dim_y
    orders = [slab_order(zp) for zp in range(NZ)]
    for slab in range(4):
        halves = []
        for hh in (yh, 1 - yh):
            pieces = []
            for zp in range(NZ):
                at = orders[zp].index(slab)
                m, low = at // 2, (at % 2) * 8
                for yy in range(2):
                    for cc in range(2):
                        pieces.append(kvr[2 * hh + yy, cc, m, zp].astype(F32)[low : low + 8])
            halves.append((jnp.concatenate(pieces[:16], 0), jnp.concatenate(pieces[16:], 0)))
        (k_here, v_here), (k_there, v_there) = halves
        keys, vals = [], []
        cos, sin = ropet_ref[0], ropet_ref[1]
        for x, y_ in (((k_here, v_here), (k_there, v_there)), ((k_there, v_there), (k_here, v_here))):
            kk = jnp.where(key_guest, y_[0], x[0])
            a, b = kk[: HD // 2], kk[HD // 2 :]
            keys.append(jnp.concatenate([a * cos - b * sin, b * cos + a * sin], 0).astype(BF16))
            vals.append(jnp.where(key_guest, y_[1], x[1]).astype(BF16))
        keys = jnp.concatenate(keys, 1)
        vals = jnp.concatenate(vals, 1)
        sc = SCALE * jnp.dot(qs[slab], keys, preferred_element_type=F32)
        sc = jnp.where(causal, sc, NEG)
        m_old = ms[slab]
        m_new = jnp.maximum(m_old, jnp.max(sc, 1, keepdims=True))
        w = jnp.where(causal, jnp.exp(sc - jnp.concatenate([m_new, m_new], 1)), 0.0)
        fix = jnp.exp(m_old - m_new)
        l = ls[slab] * fix + jnp.sum(w, 1, keepdims=True)
        acc = accs[slab] * fix + lax.dot_general(
            w.astype(BF16), vals, (((1,), (1,)), ((), ())), preferred_element_type=F32
        )
        live = jnp.where(guest, lens[1, slab : slab + 1], lens[0, slab : slab + 1])
        mixed = jnp.where(row.astype(F32) < live, acc / l, 0.0).astype(BF16)
        for i in range(8):
            rows16 = jnp.concatenate(
                [mixed[i * ROW : (i + 1) * ROW], mixed[SLAB + i * ROW : SLAB + (i + 1) * ROW]], 1
            )
            ho[i % 2, slab * 2 + i // 4, (i // 2) % 2] = rows16
        pair = pl.ds(slab * 2, 2)
        send(ho.at[1 - c, pair], hos.at[pair], hosem.at[slab], sib)
    arrived(ow.at[1], owsem.at[0])
    for slab in range(4):
        arrived(hos.at[pl.ds(slab * 2, 2)], hosem.at[slab])

    NC = 1024

    def out_proj(planes):
        a = jnp.concatenate([ho[c, zp].reshape(2 * ROW, 2 * HD) for zp in planes], 0)
        b = jnp.concatenate([hos[zp].reshape(2 * ROW, 2 * HD) for zp in planes], 0)

        for g in parts:

            def body(n, carry):
                at = pl.ds(pl.multiple_of(g * wide + n * NC, NC), NC)
                res = jnp.dot(a, ow[0, :, at], preferred_element_type=F32)
                res = res + jnp.dot(b, ow[1, :, at], preferred_element_type=F32)
                res = res.astype(BF16).reshape(len(planes), 2, ROW, NC)
                put = pl.ds(pl.multiple_of(n * NC, NC), NC)
                for i, zp in enumerate(planes):
                    part[g, zp, :, :, put] = res[i]
                return carry

            lax.fori_loop(0, wide // NC, body, 0)
        for zp in planes:
            for g in parts:
                send(part.at[g, zp, 1 - y], rby.at[g, zp], rbysem.at[g, zp], yrecv)

    def add(ref, *others):
        total = ref[...].astype(F32)
        for other in others:
            total = total + other[...].astype(F32)
        ref[...] = total.astype(BF16)

    def at(k):
        return m8(z + k)

    def by_wait(g, zp):
        arrived(rby.at[g, zp], rbysem.at[g, zp])

    out_proj([at(4), at(3), at(-3)])
    out_proj([at(2), at(-2), at(1), at(-1), z])
    for g in parts:
        turn = 1 - 2 * (g % 2)
        by_wait(g, at(4))
        add(part.at[g, at(4), y], rby.at[g, at(4)])
        send(part.at[g, at(4), y], rb4.at[g], rb4sem.at[g], step_dev[turn])
    for k in (3, 2, 1):
        for g in parts:
            turn = 1 - 2 * (g % 2)
            for d in (-turn, turn):
                zp = at(d * k)
                by_wait(g, zp)
                terms = [rby.at[g, zp]]
                if k == 3 and d == turn:
                    arrived(rb4.at[g], rb4sem.at[g])
                    terms.append(rb4.at[g])
                if k < 3:
                    arrived(rb.at[g, (1 - d) // 2, 2 - k], rbsem.at[g, (1 - d) // 2, 2 - k])
                    terms.append(rb.at[g, (1 - d) // 2, 2 - k])
                add(part.at[g, zp, y], *terms)
                i = (1 - d) // 2
                send(part.at[g, zp, y], rb.at[g, i, 3 - k], rbsem.at[g, i, 3 - k], step_dev[d])
    for g in parts:
        by_wait(g, z)
        for i in range(2):
            arrived(rb.at[g, i, 2], rbsem.at[g, i, 2])
        out_ref[:, cut[g]] = (
            part[g, z, y].astype(F32) + rby[g, z].astype(F32)
            + rb[g, 0, 2].astype(F32) + rb[g, 1, 2].astype(F32)
        ).astype(BF16)
    assert len(pending) <= 320
    for copy in pending:
        copy.wait_send()


def shards(x, qw, kvw, ow, pool, table, owner, lengths):
    cols = x.shape[1]
    wide = cols // PARTS
    kvw_t = jnp.transpose(kvw, (1, 2, 3, 0)).reshape(64, cols)
    rope, rope_t = rope_tables()
    any_ = pl.BlockSpec(memory_space=pl.ANY)
    smem = pl.BlockSpec(memory_space=pltpu.SMEM)
    vmem = pl.BlockSpec(memory_space=pltpu.VMEM)
    DMA = pltpu.SemaphoreType.DMA
    V = pltpu.VMEM
    scratch = [
        V((32, ROW, cols), BF16), V((cols, 256), BF16), V((64, cols), BF16), V((2, 256, cols), BF16),
        V((8, 8, 16, 256), BF16), V((4, 2, 8, 16, HD), BF16), V((8, 8, 16, HD), BF16), V((8, 16, HD), BF16),
        V((2, 4, 2, 2, NZ, 16, HD), BF16),
        V((64, SLAB), F32), V((2, 8, 16, SLAB), BF16), V((4, 2, 2, NZ, 16, SLAB), BF16), V((2, 8, SLAB), F32),
        V((4, 2 * SLAB, HD), BF16), V((4, 2 * SLAB, HD), F32), V((4, 2 * SLAB, HD), F32), V((4, 2 * SLAB, HD), F32),
        V((2, NZ, 2, ROW, 256), BF16), V((NZ, 2, ROW, 256), BF16),
        V((PARTS, NZ, 2, ROW, wide), BF16), V((PARTS, ROW, wide), BF16), V((PARTS, 2, 3, ROW, wide), BF16),
        V((PARTS, NZ, ROW, wide), BF16),
        DMA((320,)), DMA((5,)), DMA((PARTS, 32)), DMA((8,)), DMA((8,)), DMA((4,)), DMA((4,)), DMA((1,)),
        DMA((2, 8)), DMA((2, 8)), DMA((4,)), DMA((1,)), DMA((1,)),
        DMA((PARTS,)), DMA((PARTS, 2, 3)), DMA((PARTS, 8)),
    ]
    return pl.pallas_call(
        kernel,
        out_shape=jax.ShapeDtypeStruct((ROW, cols), BF16),
        in_specs=[any_] * 5 + [smem] * 3 + [vmem] * 2,
        out_specs=vmem,
        scratch_shapes=scratch,
        compiler_params=pltpu.CompilerParams(
            collective_id=0, has_side_effects=True, vmem_limit_bytes=56 * 1024 * 1024
        ),
    )(x, qw, kvw_t, ow, pool[0], jnp.transpose(table), owner, lengths, jnp.asarray(rope), jnp.asarray(rope_t))


def solution(mesh):
    placed = (
        P(("store", "tensor"), None),
        P(None, "tensor"),
        P(None, "tensor", None, None),
        P("tensor", None),
        P("store", "tensor", None, None, None),
        P(),
        P(),
        P("store", None),
    )
    return jax.shard_map(
        shards, mesh=mesh, in_specs=placed, out_specs=P(("store", "tensor"), None), check_vma=False
    )
```

time: 401 us -> 102 us (0.25)
  waiting for transfers between devices: 339 us -> 0 us
  Pallas kernels: 0 us -> 100 us
  matrix products: 27.5 us -> 0 us
  between operations: 15.9 us -> 0.01 us
  other arithmetic: 6.97 us -> 0 us
  local copies, waits for them, and re-layouts: 8.46 us -> 1.67 us
    reduce_scatter x1 -> x0, waiting for transfers between devices: 126 us -> none  [shards(): lax.psum_scatter(jnp.dot(heads_out, out_weight, preferred_element_type=jn...]
    all_gather x3 -> x0, waiting for transfers between devices: 125 us -> none  [the longest x1 65.2 us: shards(): kv_whole = lax.all_gather(kv_part, 'tensor', axis=1, tiled=True)]
    pallas_call x0 -> x1, Pallas kernels: none -> 100 us  [shards(): pl.pallas_call(kernel, out_shape=jax.ShapeDtypeStruct((ROW, cols), BF16),...]
    psum x1 -> x0, waiting for transfers between devices: 87.4 us -> none  [spread(): return lax.psum(block, axis)]
    dot_general x3 -> x0, matrix products: 22.3 us -> none  [the longest x1 8.29 us: shards(): jnp.dot(lax.all_gather(suffix_tokens, 'tensor', axis=0, tiled=True), stac...]
    sub x1 -> x0, matrix products: 5.13 us -> none  [attend(): exponent = jnp.exp(scores - row_max)]
  transfers between devices with their start and end apart: 5 -> 0, of which waited for: 4 -> 0; matrix products, arithmetic and copies ran while one was open for 5% -> 0% of each run, Pallas kernels for 0% -> 0%
where the time goes in v1:
time: 102 us
  Pallas kernels  100 us (98%)
  local copies, waits for them, and re-layouts  1.67 us (2%)
    pallas_call x1, Pallas kernels, shards(): pl.pallas_call(kernel, out_shape=jax.ShapeDtypeStruct((ROW, cols), BF16),...  100 us

profile of v1, /device:TPU:1, one launch (start us, length us, event | category | flops | bytes accessed | tf_op | source)
XLA Modules:
  0.0 101.8 jit_solution(16824144422806680731)
XLA Ops:
  0.0 100.1 %shard_map.100 = bf16[16,8192]{1,0:T(8,128)(2,1)} custom-call(bf16[16,8192]{1,0:T(8,128)(2,1)} %x_ref.1, bf16[8192,256]{1,0:T(8,128)(2,1)} %qw_hbm.1, bf16[64,8192]{1,0:T(8,128)(2,1)} %bitcast.5, bf16[256,8192]{1,0:T(8,128)(2,1)} %ow_hbm.1, bf16[8,8,16,256]{3,2,1,0:T(8,128)(2,1)} %bitcast.6, s32[4,32]{1,0:T(4,128)} %bitcast.7, s32[32]{0:T(128)} %own_ref.1, ...), custom_call_target="tpu_custom_call" | custom-call | tf_op jit(solution)/shard_map/pallas_call | solution.py:455
  100.1 1.7 %copy.12 = bf16[16,8192]{1,0:T(8,128)(2,1)} copy(bf16[16,8192]{1,0:T(8,128)(2,1)} %shard_map.100) | data formatting | bytes 524288

commit v2 on v1

--- a/solution.py
+++ b/solution.py
@@ -164,7 +164,7 @@
     so = z // 2
     dd = 2 * lax.rem(z, 2) - 1
     order = [so, lax.rem(so + 4 + dd, 4), lax.rem(so + 4 - dd, 4), lax.rem(so + 2, 4)]
-    KC = 1024
+    KC = 4096
 
     def rows_of(slabs, k):
         cs = pl.ds(pl.multiple_of(k * KC, KC), KC)
@@ -222,25 +222,25 @@
         slab = order[i]
         q = qs[slab]
 
-        def body(x, carry):
-            m, l, acc = carry
+        rows = 2 * SLAB
+        scores, top = [], None
+        for x in range(4):
             keys = jnp.concatenate([pb[0, x, 0].reshape(256, HD), pb[1, x, 0].reshape(256, HD)], 0)
+            sc = lax.dot_general(q, keys, (((1,), (1,)), ((), ())), preferred_element_type=F32)
+            scores.append(sc)
+            part_max = sc[:, :HD]
+            for i in range(1, 4):
+                part_max = jnp.maximum(part_max, sc[:, i * HD : (i + 1) * HD])
+            top = part_max if top is None else jnp.maximum(top, part_max)
+        m = jnp.max(top, 1, keepdims=True) * SCALE
+        l, acc = jnp.zeros((rows, HD), F32), jnp.zeros((rows, HD), F32)
+        for x in range(4):
             vals = jnp.concatenate([pb[0, x, 1].reshape(256, HD), pb[1, x, 1].reshape(256, HD)], 0)
-            sc = SCALE * lax.dot_general(
-                q, keys, (((1,), (1,)), ((), ())), preferred_element_type=F32
-            )
-            m_new = jnp.maximum(m, jnp.max(sc, 1, keepdims=True))
-            w = jnp.exp(sc - m_new)
-            fix = jnp.exp(m - m_new)
-            l = l * fix + jnp.sum(w, 1, keepdims=True)
-            acc = acc * fix + jnp.dot(w.astype(BF16), vals, preferred_element_type=F32)
-            return m_new, l, acc
-
-        rows = 2 * SLAB
-        m, l, acc = lax.fori_loop(
-            0, 4, body,
-            (jnp.full((rows, 1), NEG, F32), jnp.zeros((rows, 1), F32), jnp.zeros((rows, HD), F32)),
-        )
+            w = jnp.exp(scores[x] * SCALE - m)
+            for i in range(4):
+                l = l + w[:, i * HD : (i + 1) * HD]
+            acc = acc + jnp.dot(w.astype(BF16), vals, preferred_element_type=F32)
+        l = jnp.sum(l, 1, keepdims=True)
         ms[slab] = jnp.broadcast_to(m, (rows, HD))
         ls[slab] = jnp.broadcast_to(l, (rows, HD))
         accs[slab] = acc
@@ -305,11 +305,10 @@
     kv_wait(1)
 
     arrived(lens.at[1], lensem.at[0])
-    row = lax.rem(lax.broadcasted_iota(jnp.int32, (2 * SLAB, 2 * SLAB), 0), SLAB)
-    col = lax.broadcasted_iota(jnp.int32, (2 * SLAB, 2 * SLAB), 1)
+    row = lax.rem(lax.broadcasted_iota(jnp.int32, (2 * SLAB, SLAB), 0), SLAB)
+    col = lax.broadcasted_iota(jnp.int32, (2 * SLAB, SLAB), 1)
     guest = lax.rem(row // ROW, 4) == 2 - y
-    causal = (lax.rem(col, SLAB) <= row) & ((col >= SLAB) == guest)
-    row, guest = row[:, :SLAB], guest[:, :SLAB]
+    causal = col <= row
     lane = lax.rem(lax.broadcasted_iota(jnp.int32, (HD, SLAB), 1) // ROW, 4)
     dim_y = lax.rem(lax.broadcasted_iota(jnp.int32, (HD, SLAB), 0) // 16, 2)
     key_guest = lane == 2 - dim_y
@@ -333,18 +332,23 @@
             a, b = kk[: HD // 2], kk[HD // 2 :]
             keys.append(jnp.concatenate([a * cos - b * sin, b * cos + a * sin], 0).astype(BF16))
             vals.append(jnp.where(key_guest, y_[1], x[1]).astype(BF16))
-        keys = jnp.concatenate(keys, 1)
-        vals = jnp.concatenate(vals, 1)
-        sc = SCALE * jnp.dot(qs[slab], keys, preferred_element_type=F32)
+        q = qs[slab]
+        sc = SCALE * jnp.where(
+            guest,
+            jnp.dot(q, keys[1], preferred_element_type=F32),
+            jnp.dot(q, keys[0], preferred_element_type=F32),
+        )
         sc = jnp.where(causal, sc, NEG)
         m_old = ms[slab]
         m_new = jnp.maximum(m_old, jnp.max(sc, 1, keepdims=True))
-        w = jnp.where(causal, jnp.exp(sc - jnp.concatenate([m_new, m_new], 1)), 0.0)
+        w = jnp.where(causal, jnp.exp(sc - m_new), 0.0)
         fix = jnp.exp(m_old - m_new)
         l = ls[slab] * fix + jnp.sum(w, 1, keepdims=True)
-        acc = accs[slab] * fix + lax.dot_general(
-            w.astype(BF16), vals, (((1,), (1,)), ((), ())), preferred_element_type=F32
-        )
+        acc = accs[slab] * fix
+        for part_w, v in ((jnp.where(guest, 0.0, w), vals[0]), (jnp.where(guest, w, 0.0), vals[1])):
+            acc = acc + lax.dot_general(
+                part_w.astype(BF16), v, (((1,), (1,)), ((), ())), preferred_element_type=F32
+            )
         live = jnp.where(guest, lens[1, slab : slab + 1], lens[0, slab : slab + 1])
         mixed = jnp.where(row.astype(F32) < live, acc / l, 0.0).astype(BF16)
         for i in range(8):
@@ -376,10 +380,14 @@
                     part[g, zp, :, :, put] = res[i]
                 return carry
 
-            lax.fori_loop(0, wide // NC, body, 0)
-        for zp in planes:
-            for g in parts:
-                send(part.at[g, zp, 1 - y], rby.at[g, zp], rbysem.at[g, zp], yrecv)
+            lax.fori_loop(0, wide // NC, body, 0, unroll=True)
+            if len(planes) == 3:
+                for zp in planes:
+                    send(part.at[g, zp, 1 - y], rby.at[g, zp], rbysem.at[g, zp], yrecv)
+        if len(planes) > 3:
+            for zp in planes:
+                for g in parts:
+                    send(part.at[g, zp, 1 - y], rby.at[g, zp], rbysem.at[g, zp], yrecv)
 
     def add(ref, *others):
         total = ref[...].astype(F32)

time: 102 us -> 96.5 us (0.946)
  Pallas kernels: 100 us -> 94.7 us
    pallas_call x1, Pallas kernels: 100 us -> 94.7 us  [shards(): pl.pallas_call(kernel, out_shape=jax.ShapeDtypeStruct((ROW, cols), BF16),...]
where the time goes in v2:
time: 96.5 us; the launch traced here: 96.3 us
  Pallas kernels  94.7 us (98%)
  local copies, waits for them, and re-layouts  1.67 us (2%)
    pallas_call x1, Pallas kernels, shards(): pl.pallas_call(kernel, out_shape=jax.ShapeDtypeStruct((ROW, cols), BF16),...  94.7 us

profile of v2, /device:TPU:1, one launch (start us, length us, event | category | flops | bytes accessed | tf_op | source)
XLA Modules:
  0.0 96.3 jit_solution(5310540797805146564)
XLA Ops:
  0.0 94.7 %shard_map.100 = bf16[16,8192]{1,0:T(8,128)(2,1)} custom-call(bf16[16,8192]{1,0:T(8,128)(2,1)} %x_ref.1, bf16[8192,256]{1,0:T(8,128)(2,1)} %qw_hbm.1, bf16[64,8192]{1,0:T(8,128)(2,1)} %bitcast.5, bf16[256,8192]{1,0:T(8,128)(2,1)} %ow_hbm.1, bf16[8,8,16,256]{3,2,1,0:T(8,128)(2,1)} %bitcast.6, s32[4,32]{1,0:T(4,128)} %bitcast.7, s32[32]{0:T(128)} %own_ref.1, ...), custom_call_target="tpu_custom_call" | custom-call | tf_op jit(solution)/shard_map/pallas_call | solution.py:463
  94.7 1.7 %copy.12 = bf16[16,8192]{1,0:T(8,128)(2,1)} copy(bf16[16,8192]{1,0:T(8,128)(2,1)} %shard_map.100) | data formatting | bytes 524288

commit v3 on v2

--- a/solution.py
+++ b/solution.py
@@ -260,6 +260,7 @@
     pb[c, sx, yh, y, z] = sel[z]
     y_step(0)
     z_step(2)
+    y_step(1)
     for k in range(1, NZ):
         zz = m8(z + k)
         arrived(pb.at[c, sx, yh, y, zz], p2sem.at[zz])
@@ -267,38 +268,37 @@
         send(pb.at[c, sx, yh, y], pb.at[c, sx, yh, y], p3asem.at[yh * 2 + y], dev)
     l_ow.wait()
     send(ow.at[0], ow.at[1], owsem.at[0], sib)
-    y_step(1)
     z_step(3)
+    y_step(2)
     for dev, hh, yy in ydevs:
         arrived(pb.at[c, sx, hh, yy], p3asem.at[hh * 2 + yy])
     for k in range(1, 4):
         xx = lax.rem(sx + k, 4)
         send(pb.at[c, sx], pb.at[c, sx], p3bsem.at[sx], {"store": xx * 2 + yh})
-    y_step(2)
     l_kv.wait()
     l_q.wait()
     sib_wait(order[0])
     sib_wait(order[1])
     kv_send(0, *kv_proj(0, 1))
     q_proj(0, 1)
+    z_step(4)
+    y_step(3)
     for k in range(1, 4):
         xx = lax.rem(sx + k, 4)
         arrived(pb.at[c, xx], p3bsem.at[xx])
     send(pb.at[c], pb.at[c], p3csem.at[0], sib)
-    z_step(4)
-    y_step(3)
-    arrived(pb.at[1 - c], p3csem.at[0])
-    prefix_attn(0)
     sib_wait(order[2])
     kv0[...] = kv_proj(2)[0]
     y_step(4)
     q_proj(2)
     sib_wait(order[3])
     kv_send(1, kv0[...], kv_proj(3)[0])
+    kv_plane(0)
     q_proj(3)
-    kv_plane(0)
+    arrived(pb.at[1 - c], p3csem.at[0])
+    prefix_attn(0)
+    kv_plane(1)
     prefix_attn(1)
-    kv_plane(1)
     prefix_attn(2)
     prefix_attn(3)
     kv_wait(0)

time: 96.5 us -> 93.5 us (0.969)
  Pallas kernels: 94.7 us -> 91.7 us
    pallas_call x1, Pallas kernels: 94.7 us -> 91.7 us  [shards(): pl.pallas_call(kernel, out_shape=jax.ShapeDtypeStruct((ROW, cols), BF16),...]
where the time goes in v3:
time: 93.5 us; the launch traced here: 93.3 us
  Pallas kernels  91.7 us (98%)
  local copies, waits for them, and re-layouts  1.67 us (2%)
    pallas_call x1, Pallas kernels, shards(): pl.pallas_call(kernel, out_shape=jax.ShapeDtypeStruct((ROW, cols), BF16),...  91.7 us

profile of v3, /device:TPU:1, one launch (start us, length us, event | category | flops | bytes accessed | tf_op | source)
XLA Modules:
  0.0 93.3 jit_solution(15436384079946682865)
XLA Ops:
  0.0 91.7 %shard_map.100 = bf16[16,8192]{1,0:T(8,128)(2,1)} custom-call(bf16[16,8192]{1,0:T(8,128)(2,1)} %x_ref.1, bf16[8192,256]{1,0:T(8,128)(2,1)} %qw_hbm.1, bf16[64,8192]{1,0:T(8,128)(2,1)} %bitcast.5, bf16[256,8192]{1,0:T(8,128)(2,1)} %ow_hbm.1, bf16[8,8,16,256]{3,2,1,0:T(8,128)(2,1)} %bitcast.6, s32[4,32]{1,0:T(4,128)} %bitcast.7, s32[32]{0:T(128)} %own_ref.1, ...), custom_call_target="tpu_custom_call" | custom-call | tf_op jit(solution)/shard_map/pallas_call | solution.py:463
  91.7 1.7 %copy.12 = bf16[16,8192]{1,0:T(8,128)(2,1)} copy(bf16[16,8192]{1,0:T(8,128)(2,1)} %shard_map.100) | data formatting | bytes 524288

commit v4 on v3

--- a/solution.py
+++ b/solution.py
@@ -266,8 +266,6 @@
         arrived(pb.at[c, sx, yh, y, zz], p2sem.at[zz])
     for dev, hh, yy in ydevs:
         send(pb.at[c, sx, yh, y], pb.at[c, sx, yh, y], p3asem.at[yh * 2 + y], dev)
-    l_ow.wait()
-    send(ow.at[0], ow.at[1], owsem.at[0], sib)
     z_step(3)
     y_step(2)
     for dev, hh, yy in ydevs:
@@ -290,6 +288,8 @@
     sib_wait(order[2])
     kv0[...] = kv_proj(2)[0]
     y_step(4)
+    l_ow.wait()
+    send(ow.at[0], ow.at[1], owsem.at[0], sib)
     q_proj(2)
     sib_wait(order[3])
     kv_send(1, kv0[...], kv_proj(3)[0])

time: 93.5 us -> 93.7 us (level)
  no operation moved by 1% of the time
where the time goes in v4:
time: 93.7 us; the launch traced here: 93.6 us
  Pallas kernels  91.9 us (98%)
  local copies, waits for them, and re-layouts  1.67 us (2%)
    pallas_call x1, Pallas kernels, shards(): pl.pallas_call(kernel, out_shape=jax.ShapeDtypeStruct((ROW, cols), BF16),...  91.9 us

profile of v4, /device:TPU:1, one launch (start us, length us, event | category | flops | bytes accessed | tf_op | source)
XLA Modules:
  0.0 93.6 jit_solution(17636971677546954485)
XLA Ops:
  0.0 91.9 %shard_map.100 = bf16[16,8192]{1,0:T(8,128)(2,1)} custom-call(bf16[16,8192]{1,0:T(8,128)(2,1)} %x_ref.1, bf16[8192,256]{1,0:T(8,128)(2,1)} %qw_hbm.1, bf16[64,8192]{1,0:T(8,128)(2,1)} %bitcast.5, bf16[256,8192]{1,0:T(8,128)(2,1)} %ow_hbm.1, bf16[8,8,16,256]{3,2,1,0:T(8,128)(2,1)} %bitcast.6, s32[4,32]{1,0:T(4,128)} %bitcast.7, s32[32]{0:T(128)} %own_ref.1, ...), custom_call_target="tpu_custom_call" | custom-call | tf_op jit(solution)/shard_map/pallas_call | solution.py:463
  91.9 1.7 %copy.12 = bf16[16,8192]{1,0:T(8,128)(2,1)} copy(bf16[16,8192]{1,0:T(8,128)(2,1)} %shard_map.100) | data formatting | bytes 524288
